TPU v7x, 128 devices: a whole 4x4x4 slice. The times are simulated.
128 devices in a mesh: occ: 8 (over y, core), vir: 16 (over z, x).
Axes of the slice: x: 4, y: 4, z: 4, core: 2. Of those that a mesh axis runs over, the one named last changes fastest.
Arguments:
- amplitude: bfloat16 [16, 640, 8, 640], P(None, 'vir'), may hold values from -6 to 6
- integral: bfloat16 [8, 640, 16, 640], P(None, 'vir', 'occ'), may hold values from -0.25 to 0.25
- occ_irrep: int32 [16], replicated, may hold values from 0 to 7
- kocc_irrep: int32 [8], replicated, may hold values from 0 to 7
- vir_irrep: int32 [640], replicated, may hold values from 0 to 7, as said below
Outputs:
- residual: bfloat16 [16, 640, 16, 640], P(None, 'vir', 'occ')
Inputs may be any that keep to these rules, and one draw needn't show every extreme that they name: `occ_irrep`: D2h irrep labels. `kocc_irrep`: D2h irrep labels. D2h irrep labels, ordered by irrep: vir_irrep never falls along the virtuals. The eight irreps hold, in an order that differs from draw to draw, 160, 120, three times 2 * 40 and three times 640 // 16 virtuals, so at most 160 virtuals share one irrep, and one irrep holds exactly that many.
All inputs are finite; a program needn't handle non-finite values.
Results may differ from a plain program's by a relative error of at most 0.0051.
Values may be sent and summed in bfloat16 or wider, within the bound.
A program may use at most 128 MiB of HBM per device.

v0:
```python
import functools
import jax
import jax.numpy as jnp
from jax import lax
from jax.experimental import pallas as pl
from jax.experimental.pallas import tpu as pltpu
from jax.sharding import PartitionSpec as P

WIN = 160
FEW = 6
MESH = pl.DeviceIdType.MESH
ORDER, PLACE, BEGIN, BLOCK, GROUP, MEMBER, MOST = 0, 16, 32, 40, 72, 88, 104


def table_kernel(groups, occ_ref, virs_ref, tab):
    batch = occ_ref.shape[0]
    la = virs_ref.shape[0] // 16
    occ = [occ_ref[i] for i in range(batch)]
    places = [jnp.int32(0)] * batch
    for i in range(batch):
        for o in range(i):
            before = (occ[o] <= occ[i]).astype(jnp.int32)
            places[i] = places[i] + before
            places[o] = places[o] + (1 - before)
    below = []
    for r in range(8):
        total = jnp.int32(0)
        for o in range(batch):
            total = total + (occ[o] < r).astype(jnp.int32)
        below.append(total)
    below.append(jnp.int32(batch))
    most = jnp.int32(0)
    for r in range(8):
        most = jnp.maximum(most, below[r + 1] - below[r])
        tab[BEGIN + r] = jnp.minimum(below[r], max(batch - 3 * groups, 0))
        for d in range(4):
            tab[BLOCK + 4 * r + d] = jnp.int32(0)
    tab[MOST] = most
    for v in range(16):
        tab[BLOCK + 4 * virs_ref[la * v] + v % 4] = jnp.int32(v)
    for i in range(batch):
        tab[PLACE + i] = places[i]
        tab[ORDER + places[i]] = jnp.int32(i)
        slot = places[i] - tab[BEGIN + occ[i]]
        group = jnp.int32(0)
        for q in range(1, groups):
            group = group + (slot >= 3 * q).astype(jnp.int32)
        tab[GROUP + i] = group
        tab[MEMBER + i] = slot - 3 * group


def make_table(groups, occ_irrep, vir_irrep):
    smem = pl.BlockSpec(memory_space=pltpu.SMEM)
    return pl.pallas_call(
        functools.partial(table_kernel, groups),
        out_shape=jax.ShapeDtypeStruct((105,), jnp.int32),
        in_specs=[smem, smem],
        out_specs=smem,
        name="make_table",
    )(occ_irrep, vir_irrep)


def cycle_kernel(groups, amp_ref, w_ref, occ_ref, kocc_ref, lab_ref, virs_ref, tab, out_ref,
                 amp, panels, tk, row_wk, wk, acc, rowp, cw, comb, far, near, nearf, turned, pack_out, pack_in,
                 amp_sem, send_sem, recv_sem, far_send, far_recv, occ_send, occ_recv):
    me = lax.axis_index("vir")
    mine = lax.axis_index("occ")
    z, x = me // 4, lax.rem(me, 4)
    batch, la, nk, nv = amp.shape
    pairs = batch // 2
    here = [(x, z), (z, x)]

    amp_copies = [
        pltpu.make_async_copy(amp_ref.at[pl.ds(2 * i, 2)], amp.at[pl.ds(2 * i, 2)], amp_sem.at[i])
        for i in range(pairs)]
    for c in amp_copies:
        c.start()

    def at(h, p, q):
        p, q = lax.rem(p + 8, 4), lax.rem(q + 8, 4)
        return q * 4 + p if h == 0 else p * 4 + q

    barrier = pltpu.get_barrier_semaphore()

    @pl.loop(1, 16)
    def _(off):
        v = lax.rem(z + off // 4, 4) * 4 + lax.rem(x + off, 4)
        pl.semaphore_signal(barrier, inc=1, device_id={"vir": v}, device_id_type=MESH)

    @pl.loop(1, 8)
    def _(off):
        pl.semaphore_signal(barrier, inc=1, device_id={"occ": lax.rem(mine + off, 8)}, device_id_type=MESH)

    labs = lab_ref[...].reshape(1, nv)
    mylab = virs_ref[me * la]
    jocc = [occ_ref[2 * mine + j] for j in range(2)]

    quarter = lax.broadcasted_iota(jnp.int32, (la, nv), 1) // WIN

    def pack(h):
        both = []
        for kp in range(2):
            total = None
            for k2 in range(2):
                k = 4 * h + 2 * kp + k2
                for j in range(2):
                    want = kocc_ref[k] ^ jocc[j] ^ mylab
                    part = jnp.where(labs == want, w_ref[k, :, j, :].astype(jnp.float32), 0.0)
                    part = part + pltpu.roll(part, 2 * WIN, 1)
                    part = part + pltpu.roll(part, WIN, 1)
                    total = part if total is None else jnp.where(quarter >= 2 * k2 + j, part, total)
            both.append(total)
        panels[h, me] = jnp.concatenate(both, axis=0).astype(jnp.bfloat16)

    copies = []

    def send(h, block, rows, step, slot):
        p, q = here[h]
        ref = panels.at[h, at(h, p + block[0], q + block[1]), pl.ds(rows[0], rows[1] - rows[0])]
        c = pltpu.make_async_remote_copy(
            src_ref=ref, dst_ref=ref, send_sem=send_sem.at[h, slot], recv_sem=recv_sem.at[h, slot],
            device_id={"vir": at(h, p + step[0], q + step[1])}, device_id_type=MESH)
        c.start()
        copies.append(c)

    def arrived(h, block, rows, slot):
        p, q = here[h]
        ref = panels.at[h, at(h, p + block[0], q + block[1]), pl.ds(rows[0], rows[1] - rows[0])]
        pltpu.make_async_remote_copy(
            src_ref=ref, dst_ref=ref, send_sem=send_sem.at[h, slot], recv_sem=recv_sem.at[h, slot],
            device_id={"vir": me}, device_id_type=MESH).wait_recv()

    full = (0, 2 * la)

    def halves(h, turn):
        middle = 48 if (h + turn) % 2 else 32
        return (0, middle), (middle, 2 * la)


    def second(h, d):
        send(h, (d, 0), full, (0, 1), 4 + 4 * d)
        send(h, (d, 0), full, (0, -1), 5 + 4 * d)

    def relay(h, d):
        b = d if d < 2 else d - 4
        low, high = halves(h, d % 2)
        arrived(h, (b, -1), full, 4 + 4 * d)
        send(h, (b, -1), low, (0, 1), 6 + 4 * d)
        arrived(h, (b, 1), full, 5 + 4 * d)
        send(h, (b, 1), high, (0, -1), 7 + 4 * d)

    rows = la * nk

    def prepare(low, high):
        @pl.loop(low, high)
        def _(i):
            parts = []
            for s in range(2):
                orb = tab[ORDER + 2 * i + s]
                moved = jnp.dot(rowp[...], amp[orb].reshape(rows, nv), preferred_element_type=jnp.float32)
                left = occ_ref[orb] ^ mylab
                parts.append([
                    jnp.where(labs == (left ^ kocc_ref[k]), moved[k * la:(k + 1) * la], 0.0)
                    for k in range(nk)])
            here_rows = pl.ds(pl.multiple_of(2 * la * i, 16), 2 * la)
            for k in range(nk):
                tk[k, here_rows, :] = jnp.concatenate([parts[0][k], parts[1][k]], axis=0).astype(jnp.bfloat16)

    def multiply_row(dq, first):
        q = lax.rem(z + dq + 4, 4)
        blocks = [panels[0, 4 * q + p].astype(jnp.float32) for p in range(4)]
        for kp in range(2):
            row_wk[q, pl.ds(pl.multiple_of(256 * kp + 32 * q, 32), WIN), :] = jnp.concatenate(
                [b[kp * la:(kp + 1) * la] for b in blocks], axis=0).astype(jnp.bfloat16)
        lanes = pl.ds(pl.multiple_of(128 * q, 128), 256)
        for k2 in range(2):
            t = jnp.concatenate([tk[k2, :, lanes], tk[2 + k2, :, lanes]], axis=1)
            part = jnp.dot(t, row_wk[q, :, 256 * k2:256 * k2 + 384], preferred_element_type=jnp.float32)
            acc[k2] = part if first else acc[k2] + part

    def multiply_rest():
        for v in range(0, 16, 2):
            one, two = panels[1, v].astype(jnp.float32), panels[1, v + 1].astype(jnp.float32)
            for kp in range(2):
                wk[nv * kp + v * la:nv * kp + (v + 2) * la, :] = jnp.concatenate(
                    [one[kp * la:(kp + 1) * la], two[kp * la:(kp + 1) * la]], axis=0).astype(jnp.bfloat16)
        for k2 in range(2):
            t = jnp.concatenate([tk[4 + k2], tk[6 + k2]], axis=1)
            acc[k2] += jnp.dot(t, wk[:, 256 * k2:256 * k2 + 384], preferred_element_type=jnp.float32)

    pack(0)
    pl.semaphore_wait(barrier, 22)
    send(0, (0, 0), full, (1, 0), 0)
    send(0, (0, 0), full, (-1, 0), 1)
    second(0, 0)
    pack(1)
    send(1, (0, 0), full, (1, 0), 0)
    send(1, (0, 0), full, (-1, 0), 1)
    second(1, 0)
    r = lax.broadcasted_iota(jnp.int32, (rows, rows), 0)
    c = lax.broadcasted_iota(jnp.int32, (rows, rows), 1)
    rowp[...] = (c == lax.rem(r, la) * nk + r // la).astype(jnp.float32).astype(jnp.bfloat16)
    row_wk[...] = jnp.zeros(row_wk.shape, row_wk.dtype)
    for c in amp_copies:
        c.wait()
    prepare(0, 2)
    for h in range(2):
        low, high = halves(h, 0)
        arrived(h, (-1, 0), full, 0)
        send(h, (-1, 0), low, (1, 0), 2)
        second(h, 3)
        arrived(h, (1, 0), full, 1)
        send(h, (1, 0), high, (-1, 0), 3)
        second(h, 1)
    prepare(2, 3)
    for h in range(2):
        relay(h, 0)
    for h in range(2):
        low, high = halves(h, 0)
        arrived(h, (-2, 0), low, 2)
        arrived(h, (-2, 0), high, 3)
        second(h, 2)
    prepare(3, 5)
    for h in range(2):
        relay(h, 3)
    prepare(5, 6)
    for h in range(2):
        relay(h, 1)
    prepare(6, 8)
    for h in range(2):
        relay(h, 2)
    multiply_row(0, True)
    multiply_row(-1, False)
    multiply_row(1, False)

    def complete(h):
        for d in range(4):
            b = d if d < 2 else d - 4
            low, high = halves(h, d % 2)
            arrived(h, (b, 2), low, 6 + 4 * d)
            arrived(h, (b, 2), high, 7 + 4 * d)

    complete(0)
    multiply_row(2, False)
    complete(1)
    multiply_rest()

    whole = acc[0] + pltpu.roll(acc[1], 320, 1)
    wide = lax.broadcasted_iota(jnp.int32, whole.shape, 1)
    flatw = jnp.where(wide < 2 * WIN, whole, 0.0).astype(jnp.bfloat16).astype(jnp.float32)
    cw[...] = flatw.reshape(batch, la, 384)

    spot = lax.broadcasted_iota(jnp.int32, (batch * la, 128), 1)
    for j in range(2):
        for r in range(4):
            start = WIN * j + la * r
            tile = start // 128 * 128
            width = 128 if start + la <= tile + 128 else 256
            total = None
            for g in range(3):
                piece = flatw[g * la:, tile:tile + width]
                shift = (la * g - (start - tile)) % width
                if shift:
                    piece = pltpu.roll(piece, shift, 1)
                piece = piece[:, :128]
                if g:
                    piece = jnp.concatenate([piece, jnp.zeros((g * la, 128), jnp.float32)], axis=0)
                total = piece if g == 0 else jnp.where(spot >= g * la, piece, total)
            comb[4 * j + r] = total.reshape(batch, la, 128)

    def message(r, v):
        lab = virs_ref[v * la]
        parts = []
        for j in range(2):
            base = tab[BEGIN + (jocc[j] ^ lab ^ mylab)]
            for q in range(groups):
                parts.append(comb[4 * j + r, base + 3 * q])
        return jnp.concatenate(parts, axis=0).astype(jnp.bfloat16)

    def far_copy(off, v, source):
        return pltpu.make_async_remote_copy(
            src_ref=far.at[v], dst_ref=near.at[source], send_sem=far_send.at[off], recv_sem=far_recv.at[off],
            device_id={"vir": v}, device_id_type=MESH)

    offs = [10, 9, 11, 6, 14, 2, 8, 5, 7, 13, 15, 1, 3, 4, 12]
    for off in offs:
        v = at(0, x + off % 4, z + off // 4)
        far[v] = message(lax.rem(x + off % 4, 4), v)
        far_copy(off, v, me).start()
    near[me] = message(x, me)
    nearf[me] = near[me].astype(jnp.float32).reshape(2 * groups, la, 128)
    for off in reversed(offs):
        source = at(0, x - off % 4, z - off // 4)
        pltpu.make_async_remote_copy(
            src_ref=near.at[source], dst_ref=near.at[source], send_sem=far_send.at[off], recv_sem=far_recv.at[off],
            device_id={"vir": source}, device_id_type=MESH).wait_recv()
        nearf[source] = near[source].astype(jnp.float32).reshape(2 * groups, la, 128)

    def windows(o):
        both = []
        for j in range(2):
            wins = []
            for s in range(2):
                orb = 2 * o + s
                lab = occ_ref[orb]
                want = lab ^ mylab ^ jocc[j]
                row = groups * j + tab[GROUP + orb]
                stack = [nearf[tab[BLOCK + 4 * want + d], row] for d in range(4)]
                stack = jnp.concatenate(stack + [jnp.zeros((96, 128), jnp.float32)], axis=0).T
                for m in range(3):
                    turned[2 * j + s, m] = stack[m * la:(m + 1) * la]
                win = turned[2 * j + s, tab[MEMBER + orb]]
                wins.append(jnp.concatenate([win, jnp.zeros((la, 128), jnp.float32)], axis=1))
            both.append(wins[0] + pltpu.roll(wins[1], WIN, 1))
        return jnp.concatenate(both, axis=0).astype(jnp.bfloat16)

    def occ_copy(off, o, source):
        return pltpu.make_async_remote_copy(
            src_ref=pack_out.at[o], dst_ref=pack_in.at[source], send_sem=occ_send.at[off], recv_sem=occ_recv.at[off],
            device_id={"occ": o}, device_id_type=MESH)

    order_occ = [4, 5, 3, 2, 6, 7, 1]
    for off in order_occ:
        o = lax.rem(mine + off, 8)
        pack_out[o] = windows(o)
        occ_copy(off, o, mine).start()
    pack_in[mine] = windows(mine)

    tile_no = lax.broadcasted_iota(jnp.int32, (la, 640), 1) // WIN
    even = lax.rem(tile_no, 2) == 0

    def finish(o):
        back = pack_in[o].astype(jnp.float32)
        for j2 in range(2):
            orb = 2 * o + j2
            own_rows = cw[tab[PLACE + orb]]
            both = own_rows + back[j2 * la:(j2 + 1) * la]
            both = jnp.concatenate([both, jnp.zeros((la, 256), jnp.float32)], axis=1)
            both = both + pltpu.roll(both, 2 * WIN, 1)
            turn = pltpu.roll(both, WIN, 1)
            for j in range(2):
                want = occ_ref[orb] ^ mylab ^ jocc[j]
                row = jnp.where(even, both, turn) if j == 0 else jnp.where(even, turn, both)
                out_ref[orb, j] = jnp.where(labs == want, row, 0.0).astype(jnp.bfloat16)

    finish(mine)
    for off in reversed(order_occ):
        source = lax.rem(mine + 8 - off, 8)
        pltpu.make_async_remote_copy(
            src_ref=pack_in.at[source], dst_ref=pack_in.at[source], send_sem=occ_send.at[off],
            recv_sem=occ_recv.at[off], device_id={"occ": source}, device_id_type=MESH).wait_recv()
        finish(source)
    for c in copies:
        c.wait_send()
    for off in offs:
        far_copy(off, at(0, x + off % 4, z + off // 4), me).wait_send()
    for off in order_occ:
        occ_copy(off, lax.rem(mine + off, 8), mine).wait_send()


def residual_rows(groups, collective, amplitude, integral, occ_irrep, kocc_irrep, vir_irrep, table):
    batch, la, nk, nv = amplitude.shape
    rows = 2 * groups * la
    smem, vmem = pl.BlockSpec(memory_space=pltpu.SMEM), pl.BlockSpec(memory_space=pltpu.VMEM)
    return pl.pallas_call(
        functools.partial(cycle_kernel, groups),
        out_shape=jax.ShapeDtypeStruct((batch, 2, la, nv), jnp.bfloat16),
        in_specs=[pl.BlockSpec(memory_space=pl.ANY), vmem, smem, smem, vmem, smem, smem],
        out_specs=vmem,
        scratch_shapes=[
            pltpu.VMEM((batch, la, nk, nv), jnp.bfloat16),
            pltpu.VMEM((2, 16, 2 * la, 640), jnp.bfloat16),
            pltpu.VMEM((nk, batch * la, nv), jnp.bfloat16),
            pltpu.VMEM((4, 512, 640), jnp.bfloat16),
            pltpu.VMEM((2 * nv, 640), jnp.bfloat16),
            pltpu.VMEM((2, batch * la, 384), jnp.float32),
            pltpu.VMEM((la * nk, la * nk), jnp.bfloat16),
            pltpu.VMEM((batch, la, 384), jnp.float32),
            pltpu.VMEM((8, batch, la, 128), jnp.float32),
            pltpu.VMEM((16, rows, 128), jnp.bfloat16),
            pltpu.VMEM((16, rows, 128), jnp.bfloat16),
            pltpu.VMEM((16, 2 * groups, la, 128), jnp.float32),
            pltpu.VMEM((4, 3, la, 256), jnp.float32),
            pltpu.VMEM((8, 2 * la, 384), jnp.bfloat16),
            pltpu.VMEM((8, 2 * la, 384), jnp.bfloat16),
            pltpu.SemaphoreType.DMA((batch // 2,)),
            pltpu.SemaphoreType.DMA((2, 20)),
            pltpu.SemaphoreType.DMA((2, 20)),
            pltpu.SemaphoreType.DMA((16,)),
            pltpu.SemaphoreType.DMA((16,)),
            pltpu.SemaphoreType.DMA((8,)),
            pltpu.SemaphoreType.DMA((8,)),
        ],
        compiler_params=pltpu.CompilerParams(
            collective_id=collective, has_side_effects=True, vmem_limit_bytes=56 * 1024 * 1024),
        name="cycle_residual",
    )(amplitude, integral, occ_irrep, kocc_irrep, vir_irrep, vir_irrep, table)


def shards(amplitude, integral, occ_irrep, kocc_irrep, vir_irrep):
    table = make_table(2, occ_irrep, vir_irrep)
    args = (amplitude, integral, occ_irrep, kocc_irrep, vir_irrep)
    rows = lax.cond(
        table[MOST] <= FEW,
        lambda *a: residual_rows(2, 0, *a, table),
        lambda *a: residual_rows(6, 1, *a, make_table(6, occ_irrep, vir_irrep)),
        *args,
    )
    return jnp.transpose(rows, (0, 2, 1, 3))


def solution(mesh):
    in_specs = (P(None, "vir", None, None), P(None, "vir", "occ", None), P(), P(), P())
    out_specs = P(None, "vir", "occ", None)
    return jax.shard_map(shards, mesh=mesh, in_specs=in_specs, out_specs=out_specs, check_vma=False)
```

profile of v0, /device:TPU:1, one launch (start us, length us, event | category | flops | bytes accessed | tf_op | source)
XLA Modules:
  0.0 55.9 jit_solution(14188232232853427344)
XLA Ops:
  0.0 1.8 %make_table.3 = s32[105]{0:T(128)S(1)} custom-call(s32[16]{0:T(128)} %occ_ref.1, s32[640]{0:T(1024)} %virs_ref.1), custom_call_target="tpu_custom_call" | custom-call | tf_op jit(solution)/shard_map/make_table/pallas_call | solution.py:54
  1.8 0.6 %slice.3 = s32[1]{0:T(128)} slice(s32[105]{0:T(128)S(1)} %make_table.3), slice={[104:105]} | slice | bytes 8 | tf_op jit(solution)/shard_map/slice | solution.py:404
  3.1 50.4 %conditional.1 = (bf16[16,2,40,640]{3,2,1,0:T(8,128)(2,1)S(1)}) conditional(s32[]{:T(128)} %bitcast, (s32[16]{0:T(128)}, s32[640]{0:T(1024)}, bf16[16,40,8,640]{3,2,1,0:T(8,128)(2,1)}, bf16[8,40,2,640]{3,2,1,0:T(2,128)(2,1)}, s32[8]{0:T(128)}) %tuple.11, (bf16[16,40,8,640]{3,2,1,0:T(8,128)(2,1)}, bf16[8,40,2,640]{3,2,1,0:T(2,128)(2,1)}, s32[16]{0:T(128)}, ...), branch_computations={%region_0.0_spmd, %region_1.0_spmd} | conditional | bytes 8 | solution.py:403
  3.3 49.9 %cycle_residual.3 = bf16[16,2,40,640]{3,2,1,0:T(8,128)(2,1)S(1)} custom-call(bf16[16,40,8,640]{3,2,1,0:T(8,128)(2,1)} %get-tuple-element.35.amp_ref, bf16[8,40,2,640]{3,2,1,0:T(2,128)(2,1)} %get-tuple-element.36.w_ref, s32[16]{0:T(128)} %get-tuple-element.37.occ_ref, s32[8]{0:T(128)} %get-tuple-element.38.kocc_ref, s32[640]{0:T(1024)} %get-tuple-element.39.lab_ref.virs_ref, ...), custom_call_target="tpu_custom_call" | custom-call | tf_op jit(solution)/shard_map/cond/branch_1_fun/cycle_residual/pallas_call | solution.py:365
  53.5 2.4 %copy.8 = bf16[16,2,40,640]{3,1,2,0:T(2,128)(2,1)} copy(bf16[16,2,40,640]{3,2,1,0:T(8,128)(2,1)S(1)} %get-tuple-element.41) | data formatting | bytes 3276800 | tf_op jit(solution)/shard_map/cond | solution.py:403
where the time goes:
time: 56.1 us; the launch traced here: 55.9 us
  Pallas kernels  51.7 us (92%)
  local copies, waits for them, and re-layouts  3.01 us (5%)
  between operations  0.67 us (1%)
    pallas_call x1, Pallas kernels, residual_rows(): pl.pallas_call(functools.partial(cycle_kernel, groups), out_shape=jax.Sha...  49.9 us
    cond x1, local copies, waits for them, and re-layouts, shards(): lax.cond(table[MOST] <= FEW, lambda *a: residual_rows(2, 0, *a, table), l...  2.43 us
    pallas_call x1, Pallas kernels, make_table(): pl.pallas_call(functools.partial(table_kernel, groups), out_shape=jax.Sha...  1.82 us

commit v1 on v0

--- a/solution.py
+++ b/solution.py
@@ -178,12 +178,15 @@
             part = jnp.dot(t, row_wk[q, :, 256 * k2:256 * k2 + 384], preferred_element_type=jnp.float32)
             acc[k2] = part if first else acc[k2] + part
 
-    def multiply_rest():
-        for v in range(0, 16, 2):
+    def order_rows(half):
+        for zz in range(4):
+            v = 4 * zz + 2 * half
             one, two = panels[1, v].astype(jnp.float32), panels[1, v + 1].astype(jnp.float32)
             for kp in range(2):
-                wk[nv * kp + v * la:nv * kp + (v + 2) * la, :] = jnp.concatenate(
+                wk[pl.ds(pl.multiple_of(nv * kp + v * la, 16), 2 * la), :] = jnp.concatenate(
                     [one[kp * la:(kp + 1) * la], two[kp * la:(kp + 1) * la]], axis=0).astype(jnp.bfloat16)
+
+    def multiply_rest():
         for k2 in range(2):
             t = jnp.concatenate([tk[4 + k2], tk[6 + k2]], axis=1)
             acc[k2] += jnp.dot(t, wk[:, 256 * k2:256 * k2 + 384], preferred_element_type=jnp.float32)
@@ -229,6 +232,7 @@
     prepare(6, 8)
     for h in range(2):
         relay(h, 2)
+    order_rows(x // 2)
     multiply_row(0, True)
     multiply_row(-1, False)
     multiply_row(1, False)
@@ -243,6 +247,7 @@
     complete(0)
     multiply_row(2, False)
     complete(1)
+    order_rows(1 - x // 2)
     multiply_rest()
 
     whole = acc[0] + pltpu.roll(acc[1], 320, 1)
@@ -251,22 +256,21 @@
     cw[...] = flatw.reshape(batch, la, 384)
 
     spot = lax.broadcasted_iota(jnp.int32, (batch * la, 128), 1)
-    for j in range(2):
-        for r in range(4):
-            start = WIN * j + la * r
-            tile = start // 128 * 128
-            width = 128 if start + la <= tile + 128 else 256
-            total = None
-            for g in range(3):
-                piece = flatw[g * la:, tile:tile + width]
-                shift = (la * g - (start - tile)) % width
-                if shift:
-                    piece = pltpu.roll(piece, shift, 1)
-                piece = piece[:, :128]
-                if g:
-                    piece = jnp.concatenate([piece, jnp.zeros((g * la, 128), jnp.float32)], axis=0)
-                total = piece if g == 0 else jnp.where(spot >= g * la, piece, total)
-            comb[4 * j + r] = total.reshape(batch, la, 128)
+    def combine(j, r):
+        start = WIN * j + la * r
+        tile = start // 128 * 128
+        width = 128 if start + la <= tile + 128 else 256
+        total = None
+        for g in range(3):
+            piece = flatw[g * la:, tile:tile + width]
+            shift = (la * g - (start - tile)) % width
+            if shift:
+                piece = pltpu.roll(piece, shift, 1)
+            piece = piece[:, :128]
+            if g:
+                piece = jnp.concatenate([piece, jnp.zeros((g * la, 128), jnp.float32)], axis=0)
+            total = piece if g == 0 else jnp.where(spot >= g * la, piece, total)
+        comb[4 * j + r] = total.reshape(batch, la, 128)
 
     def message(r, v):
         lab = virs_ref[v * la]
@@ -282,19 +286,47 @@
             src_ref=far.at[v], dst_ref=near.at[source], send_sem=far_send.at[off], recv_sem=far_recv.at[off],
             device_id={"vir": v}, device_id_type=MESH)
 
+    def each(offsets, body):
+        if groups == 2:
+            for off in offsets:
+                body(off)
+        else:
+            pl.loop(1, len(offsets) + 1)(body)
+
+    def beside(off):
+        off = jnp.int32(off)
+        return lax.rem(z + off // 4, 4) * 4 + lax.rem(x + off, 4)
+
+    def behind(off):
+        off = jnp.int32(off)
+        return lax.rem(z + 4 - off // 4, 4) * 4 + lax.rem(x + 16 - off, 4)
+
     offs = [10, 9, 11, 6, 14, 2, 8, 5, 7, 13, 15, 1, 3, 4, 12]
-    for off in offs:
-        v = at(0, x + off % 4, z + off // 4)
-        far[v] = message(lax.rem(x + off % 4, 4), v)
-        far_copy(off, v, me).start()
-    near[me] = message(x, me)
+
+    for r in range(4):
+        for j in range(2):
+            combine(j, r)
+        for dz in (2, 1, 3, 0):
+            v = lax.rem(z + dz, 4) * 4 + r
+            off = 4 * dz + lax.rem(r + 4 - x, 4)
+            far[v] = message(r, v)
+            if dz:
+                far_copy(off, v, me).start()
+            else:
+                @pl.when(off != 0)
+                def _():
+                    far_copy(off, v, me).start()
+    near[me] = far[me]
     nearf[me] = near[me].astype(jnp.float32).reshape(2 * groups, la, 128)
-    for off in reversed(offs):
-        source = at(0, x - off % 4, z - off // 4)
+
+    def take_far(off):
+        source = behind(off)
         pltpu.make_async_remote_copy(
             src_ref=near.at[source], dst_ref=near.at[source], send_sem=far_send.at[off], recv_sem=far_recv.at[off],
             device_id={"vir": source}, device_id_type=MESH).wait_recv()
         nearf[source] = near[source].astype(jnp.float32).reshape(2 * groups, la, 128)
+
+    each(offs[::-1], take_far)
 
     def windows(o):
         both = []
@@ -312,7 +344,10 @@
                 win = turned[2 * j + s, tab[MEMBER + orb]]
                 wins.append(jnp.concatenate([win, jnp.zeros((la, 128), jnp.float32)], axis=1))
             both.append(wins[0] + pltpu.roll(wins[1], WIN, 1))
-        return jnp.concatenate(both, axis=0).astype(jnp.bfloat16)
+        rest = both[0][:, 256:] + pltpu.roll(both[1][:, 256:], 64, 1)
+        return jnp.concatenate(
+            [both[0][:, :128], both[1][:, :128], both[0][:, 128:256], both[1][:, 128:256], rest,
+             jnp.zeros((8, 128), jnp.float32)], axis=0).astype(jnp.bfloat16)
 
     def occ_copy(off, o, source):
         return pltpu.make_async_remote_copy(
@@ -320,21 +355,29 @@
             device_id={"occ": o}, device_id_type=MESH)
 
     order_occ = [4, 5, 3, 2, 6, 7, 1]
-    for off in order_occ:
+
+    def send_occ(off):
         o = lax.rem(mine + off, 8)
         pack_out[o] = windows(o)
         occ_copy(off, o, mine).start()
+
+    each(order_occ, send_occ)
     pack_in[mine] = windows(mine)
 
     tile_no = lax.broadcasted_iota(jnp.int32, (la, 640), 1) // WIN
     even = lax.rem(tile_no, 2) == 0
 
+    thin = lax.broadcasted_iota(jnp.int32, (la, 128), 1) < 64
+
     def finish(o):
         back = pack_in[o].astype(jnp.float32)
+        rest = back[4 * la:5 * la]
         for j2 in range(2):
             orb = 2 * o + j2
-            own_rows = cw[tab[PLACE + orb]]
-            both = own_rows + back[j2 * la:(j2 + 1) * la]
+            if j2:
+                rest = pltpu.roll(rest, 64, 1)
+            both = cw[tab[PLACE + orb]] + jnp.concatenate(
+                [back[j2 * la:(j2 + 1) * la], back[(2 + j2) * la:(3 + j2) * la], jnp.where(thin, rest, 0.0)], axis=1)
             both = jnp.concatenate([both, jnp.zeros((la, 256), jnp.float32)], axis=1)
             both = both + pltpu.roll(both, 2 * WIN, 1)
             turn = pltpu.roll(both, WIN, 1)
@@ -344,18 +387,19 @@
                 out_ref[orb, j] = jnp.where(labs == want, row, 0.0).astype(jnp.bfloat16)
 
     finish(mine)
-    for off in reversed(order_occ):
+
+    def take_occ(off):
         source = lax.rem(mine + 8 - off, 8)
         pltpu.make_async_remote_copy(
             src_ref=pack_in.at[source], dst_ref=pack_in.at[source], send_sem=occ_send.at[off],
             recv_sem=occ_recv.at[off], device_id={"occ": source}, device_id_type=MESH).wait_recv()
         finish(source)
+
+    each(order_occ[::-1], take_occ)
     for c in copies:
         c.wait_send()
-    for off in offs:
-        far_copy(off, at(0, x + off % 4, z + off // 4), me).wait_send()
-    for off in order_occ:
-        occ_copy(off, lax.rem(mine + off, 8), mine).wait_send()
+    each(offs, lambda off: far_copy(off, beside(off), me).wait_send())
+    each(order_occ, lambda off: occ_copy(off, lax.rem(mine + off, 8), mine).wait_send())
 
 
 def residual_rows(groups, collective, amplitude, integral, occ_irrep, kocc_irrep, vir_irrep, table):
@@ -381,8 +425,8 @@
             pltpu.VMEM((16, rows, 128), jnp.bfloat16),
             pltpu.VMEM((16, 2 * groups, la, 128), jnp.float32),
             pltpu.VMEM((4, 3, la, 256), jnp.float32),
-            pltpu.VMEM((8, 2 * la, 384), jnp.bfloat16),
-            pltpu.VMEM((8, 2 * la, 384), jnp.bfloat16),
+            pltpu.VMEM((8, 208, 128), jnp.bfloat16),
+            pltpu.VMEM((8, 208, 128), jnp.bfloat16),
             pltpu.SemaphoreType.DMA((batch // 2,)),
             pltpu.SemaphoreType.DMA((2, 20)),
             pltpu.SemaphoreType.DMA((2, 20)),

time: 56.1 us -> 55.9 us (level)
  no operation moved by 1% of the time
where the time goes in v1:
time: 55.9 us; the launch traced here: 55.7 us
  Pallas kernels  51.6 us (92%)
  local copies, waits for them, and re-layouts  3.01 us (5%)
  between operations  0.67 us (1%)
    pallas_call x1, Pallas kernels, residual_rows(): pl.pallas_call(functools.partial(cycle_kernel, groups), out_shape=jax.Sha...  49.8 us
    cond x1, local copies, waits for them, and re-layouts, shards(): lax.cond(table[MOST] <= FEW, lambda *a: residual_rows(2, 0, *a, table), l...  2.43 us
    pallas_call x1, Pallas kernels, make_table(): pl.pallas_call(functools.partial(table_kernel, groups), out_shape=jax.Sha...  1.82 us

profile of v1, /device:TPU:1, one launch (start us, length us, event | category | flops | bytes accessed | tf_op | source)
XLA Modules:
  0.0 55.7 jit_solution(727460649668473193)
XLA Ops:
  0.0 1.8 %make_table.3 = s32[105]{0:T(128)S(1)} custom-call(s32[16]{0:T(128)} %occ_ref.1, s32[640]{0:T(1024)} %virs_ref.1), custom_call_target="tpu_custom_call" | custom-call | tf_op jit(solution)/shard_map/make_table/pallas_call | solution.py:54
  1.8 0.6 %slice.3 = s32[1]{0:T(128)} slice(s32[105]{0:T(128)S(1)} %make_table.3), slice={[104:105]} | slice | bytes 8 | tf_op jit(solution)/shard_map/slice | solution.py:448
  3.1 50.2 %conditional.1 = (bf16[16,2,40,640]{3,2,1,0:T(8,128)(2,1)S(1)}) conditional(s32[]{:T(128)} %bitcast, (s32[16]{0:T(128)}, s32[640]{0:T(1024)}, bf16[16,40,8,640]{3,2,1,0:T(8,128)(2,1)}, bf16[8,40,2,640]{3,2,1,0:T(2,128)(2,1)}, s32[8]{0:T(128)}) %tuple.11, (bf16[16,40,8,640]{3,2,1,0:T(8,128)(2,1)}, bf16[8,40,2,640]{3,2,1,0:T(2,128)(2,1)}, s32[16]{0:T(128)}, ...), branch_computations={%region_0.0_spmd, %region_1.0_spmd} | conditional | bytes 8 | solution.py:447
  3.3 49.8 %cycle_residual.3 = bf16[16,2,40,640]{3,2,1,0:T(8,128)(2,1)S(1)} custom-call(bf16[16,40,8,640]{3,2,1,0:T(8,128)(2,1)} %get-tuple-element.35.amp_ref, bf16[8,40,2,640]{3,2,1,0:T(2,128)(2,1)} %get-tuple-element.36.w_ref, s32[16]{0:T(128)} %get-tuple-element.37.occ_ref, s32[8]{0:T(128)} %get-tuple-element.38.kocc_ref, s32[640]{0:T(1024)} %get-tuple-element.39.lab_ref.virs_ref, ...), custom_call_target="tpu_custom_call" | custom-call | tf_op jit(solution)/shard_map/cond/branch_1_fun/cycle_residual/pallas_call | solution.py:409
  53.3 2.4 %copy.8 = bf16[16,2,40,640]{3,1,2,0:T(2,128)(2,1)} copy(bf16[16,2,40,640]{3,2,1,0:T(8,128)(2,1)S(1)} %get-tuple-element.41) | data formatting | bytes 3276800 | tf_op jit(solution)/shard_map/cond | solution.py:447
